TPU v7x, 32 devices: a whole 2x2x4 slice. The times are simulated.
32 devices in a mesh: row: 4 (over z), col: 8 (over y, x, core).
Axes of the slice: x: 2, y: 2, z: 4, core: 2. Of those that a mesh axis runs over, the one named last changes fastest.
Arguments:
- sample: float32 [2, 2048, 4096], P(None, 'row', 'col'), may hold values from -6 to 6
- probe_modes: float32 [2, 2, 256, 256], replicated, may hold values from -6 to 6
- amplitude: bfloat16 [4, 8, 16, 256, 256], P('row', 'col'), may hold values from 0.5 to 3
- offsets: int32 [4, 8, 16, 2], P('row', 'col'), may hold values from 0 to 511, as said below
- counts: int32 [4, 8], P('row', 'col'), may hold values from 1 to 16, as said below
Outputs:
- new_sample: float32 [2, 2048, 4096], P(None, 'row', 'col')
- new_probe: float32 [2, 2, 256, 256], replicated
Inputs may be any that keep to these rules, and one draw needn't show every extreme that they name: `counts`: every tile has at least one live slot; some tile has exactly 16 live slots and some exactly 1. offsets[..., 0] is a row below 512, offsets[..., 1] a column below 512.
All inputs are finite; a program needn't handle non-finite values.
Results may differ from a plain program's by a relative error of at most 0.0029.
Values may be sent and summed in bfloat16 or wider, within the bound.
A program may use at most 128 MiB of HBM per device.

v0:
```python
import math

import jax
import jax.numpy as jnp
from jax import lax
from jax.sharding import PartitionSpec as P


def shifted(block, axis, distance):
    devices = range(lax.axis_size(axis))
    route = [(i - distance, i) for i in devices if i - distance in devices]
    return lax.ppermute(block, axis, route)


def dft_tables(frame):
    index = jnp.arange(frame, dtype=jnp.int32)
    product = index[:, None] * index[None, :] % frame
    angle = 2.0 * math.pi / frame * product.astype(jnp.float32)
    scale = 1.0 / math.sqrt(frame)
    return (
        (jnp.cos(angle) * scale).astype(jnp.bfloat16),
        (-jnp.sin(angle) * scale).astype(jnp.bfloat16),
    )


def apply_left(w_real, w_imag, x_real, x_imag):

    def product_of(table, field):
        return jnp.einsum("jk,mkl->mjl", table, field, preferred_element_type=jnp.float32)

    return (
        product_of(w_real, x_real) - product_of(w_imag, x_imag),
        product_of(w_real, x_imag) + product_of(w_imag, x_real),
    )


def apply_right(x_real, x_imag, w_real, w_imag):

    def product_of(field, table):
        return jnp.einsum("mjk,kl->mjl", field, table, preferred_element_type=jnp.float32)

    return (
        product_of(x_real, w_real) - product_of(x_imag, w_imag),
        product_of(x_real, w_imag) + product_of(x_imag, w_real),
    )


def make_wave(patch, probe_modes):
    probe_real = probe_modes[:, 0]
    probe_imag = probe_modes[:, 1]
    wave_real = (probe_real * patch[0] - probe_imag * patch[1]).astype(jnp.bfloat16)
    wave_imag = (probe_real * patch[1] + probe_imag * patch[0]).astype(jnp.bfloat16)
    return (wave_real, wave_imag)


def wave_gradient(wave_real, wave_imag, measured, w_real, w_imag):
    half_real, half_imag = apply_left(w_real, w_imag, wave_real, wave_imag)
    far_real, far_imag = apply_right(
        half_real.astype(jnp.bfloat16), half_imag.astype(jnp.bfloat16), w_real, w_imag
    )
    intensity = jnp.sum(far_real * far_real + far_imag * far_imag, axis=0)
    factor = 1.0 - measured.astype(jnp.float32) / jnp.maximum(jnp.sqrt(intensity), 0.25)
    corr_real = (far_real * factor).astype(jnp.bfloat16)
    corr_imag = (far_imag * factor).astype(jnp.bfloat16)
    conj_imag = -w_imag
    back_real, back_imag = apply_left(w_real, conj_imag, corr_real, corr_imag)
    grad_real, grad_imag = apply_right(
        back_real.astype(jnp.bfloat16), back_imag.astype(jnp.bfloat16), w_real, conj_imag
    )
    return (grad_real.astype(jnp.bfloat16), grad_imag.astype(jnp.bfloat16))


def add_terms(state, patch, row_at, col_at, grad_real, grad_imag, probe_modes):
    object_grad, probe_grad = state
    g_real = grad_real.astype(jnp.float32)
    g_imag = grad_imag.astype(jnp.float32)
    probe_real = probe_modes[:, 0]
    probe_imag = probe_modes[:, 1]
    term_real = jnp.sum(probe_real * g_real + probe_imag * g_imag, axis=0)
    term_imag = jnp.sum(probe_real * g_imag - probe_imag * g_real, axis=0)
    frame = patch.shape[-1]
    anchor = (jnp.int32(0), row_at, col_at)
    current = lax.dynamic_slice(object_grad, anchor, (2, frame, frame))
    object_grad = lax.dynamic_update_slice(
        object_grad, current + jnp.stack([term_real, term_imag]), anchor
    )
    probe_term_real = patch[0] * g_real + patch[1] * g_imag
    probe_term_imag = patch[0] * g_imag - patch[1] * g_real
    probe_grad = probe_grad + jnp.stack([probe_term_real, probe_term_imag], axis=1)
    return (object_grad, probe_grad)


def shards(sample, probe_modes, amplitude, offsets, counts):
    frame = probe_modes.shape[-1]
    tile_rows = sample.shape[1]
    tile_cols = sample.shape[2]
    slots = amplitude.shape[2]
    w_real, w_imag = dft_tables(frame)
    right_part = shifted(sample[:, :, :frame].astype(jnp.bfloat16), "col", -1).astype(jnp.float32)
    widened = jnp.concatenate([sample, right_part], axis=2)
    lower_part = shifted(widened[:, :frame, :].astype(jnp.bfloat16), "row", -1).astype(jnp.float32)
    extended = jnp.concatenate([widened, lower_part], axis=1)

    def slot_patch(slot):
        row_at = offsets[0, 0, slot, 0]
        col_at = offsets[0, 0, slot, 1]
        patch = lax.dynamic_slice(extended, (jnp.int32(0), row_at, col_at), (2, frame, frame))
        return (patch, row_at, col_at)

    def own_slot(slot, state):
        patch, row_at, col_at = slot_patch(slot)
        wave_real, wave_imag = make_wave(patch, probe_modes)
        grad_real, grad_imag = wave_gradient(
            wave_real, wave_imag, amplitude[0, 0, slot], w_real, w_imag
        )
        return add_terms(state, patch, row_at, col_at, grad_real, grad_imag, probe_modes)

    initial = (
        jnp.zeros((2, tile_rows + frame, tile_cols + frame), jnp.float32),
        jnp.zeros(probe_modes.shape, jnp.float32),
    )
    mine = counts[0, 0]
    object_grad, probe_grad = lax.fori_loop(0, mine, own_slot, initial)
    from_above = shifted(object_grad[:, tile_rows:, :].astype(jnp.bfloat16), "row", 1).astype(
        jnp.float32
    )
    object_grad = object_grad.at[:, :frame, :].add(from_above)
    upper_rows = object_grad[:, :tile_rows, :]
    from_left = shifted(upper_rows[:, :, tile_cols:].astype(jnp.bfloat16), "col", 1).astype(
        jnp.float32
    )
    total_grad = upper_rows[:, :, :tile_cols].at[:, :, :frame].add(from_left)
    probe_power = jnp.sum(probe_modes[:, 0] ** 2 + probe_modes[:, 1] ** 2, axis=0)
    peak = jnp.max(probe_power) + 1e-06
    new_sample = sample - total_grad / peak
    devices = lax.axis_size("row") * lax.axis_size("col")
    rate = 1.0 / math.sqrt(devices * slots)
    summed = lax.psum(probe_grad, ("row", "col"))
    new_probe = probe_modes - rate * summed
    return (new_sample, new_probe)


def solution(mesh):
    in_specs = (
        P(None, "row", "col"),
        P(),
        P("row", "col", None, None, None),
        P("row", "col", None, None),
        P("row", "col"),
    )
    out_specs = (P(None, "row", "col"), P())
    return jax.shard_map(shards, mesh=mesh, in_specs=in_specs, out_specs=out_specs, check_vma=False)
```

profile of v0, /device:TPU:0, one launch (start us, length us, event | category | flops | bytes accessed | tf_op | source)
XLA Modules:
  0.0 763.0 jit_solution(8157721249052995429)
XLA Ops:
  7.2 1.4 slice.142
  8.6 1.3 collective-permute-start
  9.9 2.5 collective-permute-done
  13.5 1.3 collective-permute-start.1
  14.9 15.7 %collective-permute-done.1 = bf16[2,256,768]{2,1,0:T(8,128)(2,1)S(1)} collective-permute-done((bf16[2,256,768]{2,1,0:T(8,128)(2,1)}, bf16[2,256,768]{2,1,0:T(8,128)(2,1)S(1)}, u32[]{:S(2)}, u32[]{:S(2)}) %collective-permute-start.1) | collective-permute-done | bytes 786464 | tf_op jit(solution)/shard_map/ppermute | solution.py:12
  30.8 4.1 pad_maximum_fusion
  34.9 2.5 broadcast_in_dim.4
  37.4 35.5 %while.17 = (s32[]{:T(128)}, f32[2,768,768]{2,1,0:T(8,128)}, f32[2,2,256,256]{3,2,0,1:T(8,128)S(1)}, s32[]{:T(128)}, s32[1,1,16,2]{2,3,1,0:T(2,128)S(1)}, /*inde...) while((s32[]{:T(128)}, f32[2,768,768]{2,1,0:T(8,128)}, ...), condition=%wide.region_4.5_spmd.clone.clone, body=%wide.region_0.4_spmd.clone.clone.sunk | while | flops 1099235328 | bytes 31326496 | solution.py:123
  42.7 1.3 dynamic-slice_bitcast_fusion.3
  56.0 1.2 fusion.240
  63.2 1.4 add_bitcast_fusion.2
  64.9 1.4 maximum_add_fusion.4
  66.3 6.0 dynamic_update_slice.7
  72.9 1.5 slice.140
  74.4 112.2 %collective-permute-start.2 = (bf16[2,256,768]{2,1,0:T(8,128)(2,1)S(1)}, bf16[2,256,768]{2,1,0:T(8,128)(2,1)}, u32[]{:S(2)}, u32[]{:S(2)}) collective-permute-start(bf16[2,256,768]{2,1,0:T(8,128)(2,1)S(1)} %slice.140), channel_id=1, source_target_pairs={{0,8},{8,16},{16,24},{1,9},{9,17},{17,25},{2,10},{10,18},{18,26},{... | collective-permute-start | bytes 2359304 | tf_op jit(solution)/shard_map/ppermute | solution.py:12
  187.7 7.5 collective-permute-done.2
  195.2 2.9 add_dynamic-update-slice_fusion
  198.1 1.3 slice.141
  199.4 360.7 %collective-permute-start.3 = (bf16[2,512,256]{2,1,0:T(8,128)(2,1)S(1)}, bf16[2,512,256]{2,1,0:T(8,128)(2,1)S(1)}, u32[]{:S(2)}, u32[]{:S(2)}) collective-permute-start(bf16[2,512,256]{2,1,0:T(8,128)(2,1)S(1)} %slice.141), channel_id=1, source_target_pairs={{0,1},{1,2},{2,3},{3,4},{4,5},{5,6},{6,7},{8,9},{9,10},{10,11},{11... | collective-permute-start | bytes 1572872 | tf_op jit(solution)/shard_map/ppermute | solution.py:12
  561.5 186.8 %all-reduce.2.cloned.1.call-done = f32[2,2,256,256]{3,2,1,0:T(8,128)} async-done(((f32[2,2,256,256]{3,2,1,0:T(8,128)}), f32[2,2,256,256]{3,2,1,0:T(8,128)}) %all-reduce.2.cloned.1.call-update) | async-done | bytes 1048592 | tf_op jit(solution)/shard_map/psum | solution.py:138
  748.3 2.3 multiply_subtract_fusion
  750.7 1.8 slice.120
  752.5 1.5 fusion.144
  754.4 1.8 divide_subtract_fusion
  (39 shorter events, 22.3 us)
Async XLA Ops:
  7.2 5.4 copy-start
  7.2 741.2 %all-reduce.2.cloned.1.call-start = ((), (), s32[]{:S(2)}) async-start(), calls=%async_computation | async-start | bytes 2097152 | tf_op jit(solution)/shard_map/psum | solution.py:138
  8.6 3.8 collective-permute-start
  12.5 2.3 copy-start.2
  13.5 17.1 %collective-permute-start.1 = (bf16[2,256,768]{2,1,0:T(8,128)(2,1)}, bf16[2,256,768]{2,1,0:T(8,128)(2,1)S(1)}, u32[]{:S(2)}, u32[]{:S(2)}) collective-permute-start(bf16[2,256,768]{2,1,0:T(8,128)(2,1)} %fusion.143), channel_id=1, source_target_pairs={{8,0},{16,8},{24,16},{9,1},{17,9},{25,17},{10,2},{18,10},{26,18},{... | collective-permute-start | bytes 2359304 | tf_op jit(solution)/shard_map/ppermute | solution.py:12
  34.9 2.6 copy-start.4
  74.4 120.8 %collective-permute-start.2 = (bf16[2,256,768]{2,1,0:T(8,128)(2,1)S(1)}, bf16[2,256,768]{2,1,0:T(8,128)(2,1)}, u32[]{:S(2)}, u32[]{:S(2)}) collective-permute-start(bf16[2,256,768]{2,1,0:T(8,128)(2,1)S(1)} %slice.140), channel_id=1, source_target_pairs={{0,8},{8,16},{16,24},{1,9},{9,17},{17,25},{2,10},{10,18},{18,26},{... | collective-permute-start | bytes 2359304 | tf_op jit(solution)/shard_map/ppermute | solution.py:12
  187.7 372.4 %copy-start.3 = (f32[2,2,256,256]{3,2,1,0:T(8,128)S(1)}, f32[2,2,256,256]{3,2,1,0:T(8,128)}, u32[]{:S(2)}) copy-start(f32[2,2,256,256]{3,2,1,0:T(8,128)} %param.12) | copy-start | bytes 3145732
  199.4 553.0 %collective-permute-start.3 = (bf16[2,512,256]{2,1,0:T(8,128)(2,1)S(1)}, bf16[2,512,256]{2,1,0:T(8,128)(2,1)S(1)}, u32[]{:S(2)}, u32[]{:S(2)}) collective-permute-start(bf16[2,512,256]{2,1,0:T(8,128)(2,1)S(1)} %slice.141), channel_id=1, source_target_pairs={{0,1},{1,2},{2,3},{3,4},{4,5},{5,6},{6,7},{8,9},{9,10},{10,11},{11... | collective-permute-start | bytes 1572872 | tf_op jit(solution)/shard_map/ppermute | solution.py:12
  752.5 1.9 copy-start.1
Sparse Core Ops, SparseCore 0:
  187.8 560.4 all-reduce.1
where the time goes:
time: 768 us; the launch traced here: 763 us
  starting transfers between devices  476 us (62%)
  waiting for transfers between devices  213 us (28%)
  matrix products  19.3 us (3%)
  local copies, waits for them, and re-layouts  18 us (2%)
  other arithmetic  17.4 us (2%)
  between operations  14.8 us (2%)
    ppermute x4, starting transfers between devices, shifted(): return lax.ppermute(block, axis, route)  475 us
    psum x1, waiting for transfers between devices, shards(): summed = lax.psum(probe_grad, ('row', 'col'))  187 us
    ppermute x4, waiting for transfers between devices, shifted(): return lax.ppermute(block, axis, route)  25.7 us
  transfers between devices with their start and end apart: 5, of which 4 were waited for; matrix products, arithmetic and copies ran while one was open for 1% of the time, Pallas kernels for 0%

commit v1 on v0

v1 whole, which is shorter than its diff:
```python
import math

import jax
import jax.numpy as jnp
import ml_dtypes
import numpy as np
from jax import lax
from jax.experimental import pallas as pl
from jax.experimental.pallas import tpu as pltpu
from jax.sharding import PartitionSpec as P

LANES = 128
CHUNK = 16


def shifted(block, axes, distances):
    sizes = [lax.axis_size(a) for a in axes]
    route = []
    for flat in range(math.prod(sizes)):
        at = np.unravel_index(flat, sizes)
        to = [int(i) + d for i, d in zip(at, distances)]
        if all(0 <= i < n for i, n in zip(to, sizes)):
            route.append((flat, int(np.ravel_multi_index(to, sizes))))
    return lax.ppermute(block, axes, route)


def tables(frame):
    index = np.arange(frame)
    angle = 2.0 * math.pi / frame * ((index[:, None] * index[None, :]) % frame)
    scale = 1.0 / math.sqrt(frame)
    w_real, w_imag = np.cos(angle) * scale, -np.sin(angle) * scale

    def block(first):
        real, imag = w_real[first::2, : frame // 2], w_imag[first::2, : frame // 2]
        return np.block([[real, -imag], [imag, real]])

    even, odd = block(0), block(1)
    order = np.concatenate([index[0::2], index[1::2]])
    pick = np.eye(frame)[order]
    stack = np.stack([even, odd, even.T, odd.T, pick, pick.T])
    return stack.astype(np.float32).astype(ml_dtypes.bfloat16)


def gradient_kernel(
    offsets, counts, table, sample, right, below, corner, probe, amplitude,
    main_out, right_out, below_out, corner_out, probe_out,
    ext, acc, patch, xs, ys, zs, gs,
):
    rows, cols = sample.shape[1:]
    frame = probe.shape[-1]
    half = frame // 2
    own = cols // LANES
    wide = ext.shape[1]
    f32, bf16 = jnp.float32, jnp.bfloat16

    for c in range(2):
        for j in range(own):
            at = slice(j * LANES, (j + 1) * LANES)
            ext[c, j, :rows, :] = sample[c, :, at]
            ext[c, j, rows:, :] = below[c, :, at].astype(f32)
        for j in range(own, wide):
            at = slice((j - own) * LANES, (j - own + 1) * LANES)
            ext[c, j, :rows, :] = right[c, :, at].astype(f32)
            ext[c, j, rows:, :] = corner[c, :, at].astype(f32)
    acc[...] = jnp.zeros_like(acc)
    probe_out[...] = jnp.zeros_like(probe_out)

    def dot(a, b):
        return jnp.dot(a, b, preferred_element_type=f32)

    def visit(slot, carry):
        row_at = offsets[2 * slot]
        col_at = offsets[2 * slot + 1]
        panel = col_at // LANES
        lane_at = col_at % LANES
        back_by = lax.rem(LANES - lane_at, LANES)
        lane = lax.broadcasted_iota(jnp.int32, (CHUNK, LANES), 1)
        inside = lane < LANES - lane_at
        after = lane >= lane_at

        measured = dot(table[4], amplitude[slot]).astype(bf16)
        measured = dot(measured, table[5])

        def window(c, t):
            parts = [
                pltpu.roll(ext[c, panel + j, pl.ds(row_at + t, CHUNK), :], back_by, 1)
                for j in range(3)
            ]
            return [jnp.where(inside, parts[j], parts[j + 1]) for j in range(2)]

        for t in range(0, half, CHUNK):
            waves = []
            for h in range(2):
                u = h * half + t
                o_real, o_imag = window(0, u), window(1, u)
                wave = {}
                for j in range(2):
                    at = slice(j * LANES, (j + 1) * LANES)
                    patch[0, u : u + CHUNK, at] = o_real[j]
                    patch[1, u : u + CHUNK, at] = o_imag[j]
                    for m in range(2):
                        p_real = probe[m, 0, u : u + CHUNK, at]
                        p_imag = probe[m, 1, u : u + CHUNK, at]
                        wave[m, j, 0] = p_real * o_real[j] - p_imag * o_imag[j]
                        wave[m, j, 1] = p_real * o_imag[j] + p_imag * o_real[j]
                waves.append(wave)
            for m in range(2):
                for j in range(2):
                    at = slice(m * frame + j * LANES, m * frame + (j + 1) * LANES)
                    for c in range(2):
                        low, high = waves[0][m, j, c], waves[1][m, j, c]
                        to = slice(c * half + t, c * half + t + CHUNK)
                        xs[0, to, at] = (low + high).astype(bf16)
                        xs[1, to, at] = (low - high).astype(bf16)

        for p in range(2):
            product = dot(table[p], xs[p])
            for m in range(2):
                to = slice((2 * p + m) * half, (2 * p + m + 1) * half)
                for c in range(2):
                    value = product[c * half : (c + 1) * half, m * frame : (m + 1) * frame]
                    low, high = value[:, :half], value[:, half:]
                    at = slice(c * half, (c + 1) * half)
                    ys[0, to, at] = (low + high).astype(bf16)
                    ys[1, to, at] = (low - high).astype(bf16)

        for q in range(2):
            far = dot(ys[q], table[2 + q])
            for p in range(2):
                rows_of = [slice((2 * p + m) * half, (2 * p + m + 1) * half) for m in range(2)]
                fields = [[far[r, :half], far[r, half:]] for r in rows_of]
                intensity = sum(f[0] * f[0] + f[1] * f[1] for f in fields)
                level = measured[p * half : (p + 1) * half, q * half : (q + 1) * half]
                factor = 1.0 - level * lax.rsqrt(jnp.maximum(intensity, 0.0625))
                for m in range(2):
                    at = slice(m * frame + q * half, m * frame + (q + 1) * half)
                    for c in range(2):
                        zs[p, c * half : (c + 1) * half, at] = (fields[m][c] * factor).astype(bf16)

        from_even = dot(table[2], zs[0])
        from_odd = dot(table[3], zs[1])
        for h, back in enumerate((from_even + from_odd, from_even - from_odd)):
            for m in range(2):
                to = slice((2 * h + m) * half, (2 * h + m + 1) * half)
                for q in range(2):
                    at = slice(m * frame + q * half, m * frame + (q + 1) * half)
                    for c in range(2):
                        gs[q, to, c * half : (c + 1) * half] = back[
                            c * half : (c + 1) * half, at
                        ].astype(bf16)

        grad_even = dot(gs[0], table[0])
        grad_odd = dot(gs[1], table[1])
        for t in range(0, frame, CHUNK):
            h, u = divmod(t, half)
            terms = [[None, None], [None, None]]
            for j in range(2):
                at = slice(j * LANES, (j + 1) * LANES)
                here = slice(t, t + CHUNK)
                o_real, o_imag = patch[0, here, at], patch[1, here, at]
                for m in range(2):
                    of = slice((2 * h + m) * half + u, (2 * h + m) * half + u + CHUNK)
                    g = []
                    for c in range(2):
                        e = grad_even[of, c * half : (c + 1) * half]
                        o = grad_odd[of, c * half : (c + 1) * half]
                        g.append(e + o if j == 0 else e - o)
                    p_real, p_imag = probe[m, 0, here, at], probe[m, 1, here, at]
                    add_real = p_real * g[0] + p_imag * g[1]
                    add_imag = p_real * g[1] - p_imag * g[0]
                    terms[0][j] = add_real if m == 0 else terms[0][j] + add_real
                    terms[1][j] = add_imag if m == 0 else terms[1][j] + add_imag
                    probe_out[m, 0, here, at] += o_real * g[0] + o_imag * g[1]
                    probe_out[m, 1, here, at] += o_real * g[1] - o_imag * g[0]
            for c in range(2):
                first = pltpu.roll(terms[c][0], lane_at, 1)
                second = pltpu.roll(terms[c][1], lane_at, 1)
                spread = (
                    jnp.where(after, first, 0.0),
                    jnp.where(after, second, first),
                    jnp.where(after, 0.0, second),
                )
                for j in range(3):
                    acc[c, panel + j, pl.ds(row_at + t, CHUNK), :] += spread[j]
        return carry

    lax.fori_loop(0, counts[0], visit, 0)

    for c in range(2):
        for j in range(own):
            at = slice(j * LANES, (j + 1) * LANES)
            main_out[c, :, at] = acc[c, j, :rows, :]
            below_out[c, :, at] = acc[c, j, rows:, :].astype(bf16)
        for j in range(own, wide):
            at = slice((j - own) * LANES, (j - own + 1) * LANES)
            right_out[c, :, at] = acc[c, j, :rows, :].astype(bf16)
            corner_out[c, :, at] = acc[c, j, rows:, :].astype(bf16)


def shards(sample, probe_modes, amplitude, offsets, counts):
    frame = probe_modes.shape[-1]
    rows, cols = sample.shape[1:]
    slots = amplitude.shape[2]
    f32, bf16 = jnp.float32, jnp.bfloat16
    edge = sample.astype(bf16)
    right = shifted(edge[:, :, :frame], ("row", "col"), (0, -1))
    below = shifted(edge[:, :frame, :], ("row", "col"), (-1, 0))
    corner = shifted(edge[:, :frame, :frame], ("row", "col"), (-1, -1))
    panels = (cols + frame) // LANES
    shape = jax.ShapeDtypeStruct
    vmem = pl.BlockSpec(memory_space=pltpu.VMEM)
    smem = pl.BlockSpec(memory_space=pltpu.SMEM)
    main, right_grad, below_grad, corner_grad, probe_grad = pl.pallas_call(
        gradient_kernel,
        out_shape=(
            shape((2, rows, cols), f32),
            shape((2, rows, frame), bf16),
            shape((2, frame, cols), bf16),
            shape((2, frame, frame), bf16),
            shape(probe_modes.shape, f32),
        ),
        in_specs=[smem, smem] + [vmem] * 7,
        out_specs=(vmem,) * 5,
        scratch_shapes=[
            pltpu.VMEM((2, panels, rows + frame, LANES), f32),
            pltpu.VMEM((2, panels, rows + frame, LANES), f32),
            pltpu.VMEM((2, frame, frame), f32),
            pltpu.VMEM((2, frame, 2 * frame), bf16),
            pltpu.VMEM((2, 2 * frame, frame), bf16),
            pltpu.VMEM((2, frame, 2 * frame), bf16),
            pltpu.VMEM((2, 2 * frame, frame), bf16),
        ],
        compiler_params=pltpu.CompilerParams(vmem_limit_bytes=48 * 1024 * 1024),
    )(
        offsets.reshape(-1), counts.reshape(-1), jnp.asarray(tables(frame)), sample,
        right, below, corner, probe_modes, amplitude.reshape(slots, frame, frame),
    )
    from_left = shifted(right_grad, ("row", "col"), (0, 1))
    from_above = shifted(below_grad, ("row", "col"), (1, 0))
    from_both = shifted(corner_grad, ("row", "col"), (1, 1))
    summed = lax.psum(probe_grad, ("row", "col"))

    def placed(block):
        tall, broad = rows - block.shape[1], cols - block.shape[2]
        return jnp.pad(block.astype(f32), ((0, 0), (0, tall), (0, broad)))

    total = main + placed(from_left) + placed(from_above) + placed(from_both)
    power = jnp.sum(probe_modes[:, 0] ** 2 + probe_modes[:, 1] ** 2, axis=0)
    new_sample = sample - total / (jnp.max(power) + 1e-06)
    devices = lax.axis_size("row") * lax.axis_size("col")
    new_probe = probe_modes - (1.0 / math.sqrt(devices * slots)) * summed
    return (new_sample, new_probe)


def solution(mesh):
    in_specs = (
        P(None, "row", "col"),
        P(),
        P("row", "col", None, None, None),
        P("row", "col", None, None),
        P("row", "col"),
    )
    out_specs = (P(None, "row", "col"), P())
    return jax.shard_map(shards, mesh=mesh, in_specs=in_specs, out_specs=out_specs, check_vma=False)
```

time: 768 us -> 211 us (0.27)
  starting transfers between devices: 476 us -> 32.4 us
  waiting for transfers between devices: 213 us -> 133 us
  matrix products: 19.3 us -> 0 us
  Pallas kernels: 0 us -> 15.1 us
  local copies, waits for them, and re-layouts: 18 us -> 3.49 us
    ppermute x4 -> x6, starting transfers between devices: 475 us -> 32.4 us  [shifted(): return lax.ppermute(block, axes, route)]
    psum x1, waiting for transfers between devices: 187 us -> 116 us  [shards(): summed = lax.psum(probe_grad, ('row', 'col'))]
    dot_general x16 -> x0, matrix products: 19.3 us -> none  [the longest x8 9.77 us: product_of(): jnp.einsum('mjk,kl->mjl', field, table, preferred_element_type=jnp.float32)]
    pallas_call x0 -> x1, Pallas kernels: none -> 15.1 us  [shards(): pl.pallas_call(gradient_kernel, out_shape=(shape((2, rows, cols), f32), s...]
    ppermute x4 -> x6, waiting for transfers between devices: 25.7 us -> 17.3 us  [shifted(): return lax.ppermute(block, axes, route)]
  transfers between devices with their start and end apart: 5 -> 7, of which waited for: 4 -> 2; matrix products, arithmetic and copies ran while one was open for 1% -> 3% of each run, Pallas kernels for 0% -> 0%
where the time goes in v1:
time: 211 us; the launch traced here: 210 us
  waiting for transfers between devices  133 us (63%)
  starting transfers between devices  32.4 us (15%)
  between operations  15.4 us (7%)
  Pallas kernels  15.1 us (7%)
  other arithmetic  9.82 us (5%)
  local copies, waits for them, and re-layouts  3.49 us (2%)
    psum x1, waiting for transfers between devices, shards(): summed = lax.psum(probe_grad, ('row', 'col'))  116 us
    ppermute x6, starting transfers between devices, shifted(): return lax.ppermute(block, axes, route)  32.4 us
    ppermute x6, waiting for transfers between devices, shifted(): return lax.ppermute(block, axes, route)  17.3 us
    pallas_call x1, Pallas kernels, shards(): pl.pallas_call(gradient_kernel, out_shape=(shape((2, rows, cols), f32), s...  15.1 us
  transfers between devices with their start and end apart: 7, of which 2 were waited for; matrix products, arithmetic and copies ran while one was open for 3% of the time, Pallas kernels for 0%

profile of v1, /device:TPU:0, one launch (start us, length us, event | category | flops | bytes accessed | tf_op | source)
XLA Modules:
  0.0 209.6 jit_solution(3949640355586819985)
XLA Ops:
  7.2 0.0 all-reduce.5.cloned.1.call-start
  7.2 1.7 convert_element_type.7
  8.9 0.0 copy-start.6
  9.0 0.0 copy-start.1
  9.0 0.8 slice.20
  9.8 1.3 collective-permute-start
  11.1 0.8 slice.21
  11.9 1.3 collective-permute-start.1
  13.2 1.3 collective-permute-start.2
  15.2 0.1 copy.10
  15.3 0.1 reshape.16.offsets
  15.4 17.3 %collective-permute-done.2.corner = bf16[2,256,256]{2,1,0:T(8,128)(2,1)S(1)} collective-permute-done((bf16[2,256,256]{2,1,0:T(8,128)(2,1)S(1)}, bf16[2,256,256]{2,1,0:T(8,128)(2,1)S(1)}, u32[]{:S(2)}, u32[]{:S(2)}) %collective-permute-start.2) | collective-permute-done | bytes 262176 | tf_op jit(solution)/shard_map/ppermute | solution.py:24
  32.7 15.1 %shard_map.77 = (f32[2,512,512]{2,1,0:T(8,128)}, bf16[2,512,256]{2,1,0:T(8,128)(2,1)S(1)}, bf16[2,256,512]{2,1,0:T(8,128)(2,1)S(1)}, bf16[2,256,256]{2,1,0:T(8,128)(2,1)S(1)}, f32[2,2,256,256]{3,2,1,0:T(8,128)}) custom-call(s32[32]{0:T(128)S(1)} %reshape.16.offsets, s32[1]{0:T(128)} %bitcast.4.counts, bf16[6,256,256]{2,1,0:T(8,128)(2,1)S(1)} %copy-done.1, ...), custom_call_target="tpu_custom_call" | custom-call | tf_op jit(solution)/shard_map/pallas_call | solution.py:213
  47.8 0.8 copy-done.2
  48.6 0.8 copy-done.3
  49.4 0.0 all-reduce.5.cloned.1.call-update
  49.4 24.3 %collective-permute-start.3 = (bf16[2,512,256]{2,1,0:T(8,128)(2,1)}, bf16[2,512,256]{2,1,0:T(8,128)(2,1)}, u32[]{:S(2)}, u32[]{:S(2)}) collective-permute-start(bf16[2,512,256]{2,1,0:T(8,128)(2,1)} %copy-done.3), channel_id=1, source_target_pairs={{0,1},{1,2},{2,3},{3,4},{4,5},{5,6},{6,7},{8,9},{9,10},{10,11},{11... | collective-permute-start | bytes 1572872 | tf_op jit(solution)/shard_map/ppermute | solution.py:24
  73.7 2.2 %collective-permute-start.4 = (bf16[2,256,512]{2,1,0:T(8,128)(2,1)}, bf16[2,256,512]{2,1,0:T(8,128)(2,1)}, u32[]{:S(2)}, u32[]{:S(2)}) collective-permute-start(bf16[2,256,512]{2,1,0:T(8,128)(2,1)} %copy-done.2), channel_id=1, source_target_pairs={{0,8},{1,9},{2,10},{3,11},{4,12},{5,13},{6,14},{7,15},{8,16},{9,17... | collective-permute-start | bytes 1572872 | tf_op jit(solution)/shard_map/ppermute | solution.py:24
  75.9 0.8 add_reduce_fusion
  76.7 1.6 reduce_max.9
  78.9 2.0 collective-permute-start.5
  80.9 116.1 %all-reduce.5.cloned.1.call-done = f32[2,2,256,256]{3,2,1,0:T(8,128)} async-done(((f32[2,2,256,256]{3,2,1,0:T(8,128)}), f32[2,2,256,256]{3,2,1,0:T(8,128)}) %all-reduce.5.cloned.1.call-update) | async-done | bytes 1048592 | tf_op jit(solution)/shard_map/psum | solution.py:241
  197.0 2.5 %multiply_subtract_fusion = f32[2,2,256,256]{3,2,1,0:T(8,128)} fusion(f32[2,2,256,256]{3,2,1,0:T(8,128)S(1)} %copy-done, f32[2,2,256,256]{3,2,1,0:T(8,128)} %all-reduce.5.cloned.1.call-done), kind=kLoop, calls=%fused_computation.1 | loop fusion | flops 524288 | bytes 3145728 | tf_op jit(solution)/shard_map/sub | solution.py:251
  199.5 3.2 %divide_subtract_fusion = f32[2,512,512]{2,1,0:T(8,128)} fusion(f32[2,512,512]{2,1,0:T(8,128)S(1)} %copy-done.4, f32[2,512,512]{2,1,0:T(8,128)S(1)} %copy-done.5, f32[]{:T(128)S(6)} %add.28, bf16[2,256,256]{2,1,0:T(8,128)(2,1)} %collective-permute-done.5, bf16[2,256,512]{2,1,0:T(8,128)(2,1)} %collective-permute-done.4, ...), kind=kLoop, calls=%fused_computation | loop fusion | flops 4194304 | bytes 7602180 | tf_op jit(solution)/shard_map/sub | solution.py:249
  (16 shorter events, 0.1 us)
Async XLA Ops:
  7.2 189.8 %all-reduce.5.cloned.1.call-start = ((), (), s32[]{:S(2)}) async-start(), calls=%async_computation | async-start | bytes 2097152 | tf_op jit(solution)/shard_map/psum | solution.py:241
  8.9 6.2 %copy-start.6 = (s32[1,1,16,2]{2,3,1,0:T(2,128)S(1)}, s32[1,1,16,2]{2,3,1,0:T(2,128)}, u32[]{:S(2)}) copy-start(s32[1,1,16,2]{2,3,1,0:T(2,128)} %param.9) | copy-start | bytes 388
  8.9 23.7 %copy-start = (f32[2,2,256,256]{3,2,1,0:T(8,128)S(1)}, f32[2,2,256,256]{3,2,1,0:T(8,128)}, u32[]{:S(2)}) copy-start(f32[2,2,256,256]{3,2,1,0:T(8,128)} %probe.1) | copy-start | bytes 3145732
  9.0 23.7 %copy-start.1 = (bf16[6,256,256]{2,1,0:T(8,128)(2,1)S(1)}, bf16[6,256,256]{2,1,0:T(8,128)(2,1)}, u32[]{:S(2)}) copy-start(bf16[6,256,256]{2,1,0:T(8,128)(2,1)} %constant.14.clone.table) | copy-start | bytes 2359300
  9.8 22.8 %collective-permute-start = (bf16[2,512,256]{2,1,0:T(8,128)(2,1)}, bf16[2,512,256]{2,1,0:T(8,128)(2,1)S(1)}, u32[]{:S(2)}, u32[]{:S(2)}) collective-permute-start(bf16[2,512,256]{2,1,0:T(8,128)(2,1)} %slice.20), channel_id=1, source_target_pairs={{1,0},{2,1},{3,2},{4,3},{5,4},{6,5},{7,6},{9,8},{10,9},{11,10},{12... | collective-permute-start | bytes 1572872 | tf_op jit(solution)/shard_map/ppermute | solution.py:24
  11.9 20.7 %collective-permute-start.1 = (bf16[2,256,512]{2,1,0:T(8,128)(2,1)}, bf16[2,256,512]{2,1,0:T(8,128)(2,1)S(1)}, u32[]{:S(2)}, u32[]{:S(2)}) collective-permute-start(bf16[2,256,512]{2,1,0:T(8,128)(2,1)} %slice.21), channel_id=1, source_target_pairs={{8,0},{9,1},{10,2},{11,3},{12,4},{13,5},{14,6},{15,7},{16,8},{17,9... | collective-permute-start | bytes 1572872 | tf_op jit(solution)/shard_map/ppermute | solution.py:24
  13.2 19.4 %collective-permute-start.2 = (bf16[2,256,256]{2,1,0:T(8,128)(2,1)S(1)}, bf16[2,256,256]{2,1,0:T(8,128)(2,1)S(1)}, u32[]{:S(2)}, u32[]{:S(2)}) collective-permute-start(bf16[2,256,256]{2,1,0:T(8,128)(2,1)S(1)} %slice.22), channel_id=1, source_target_pairs={{9,0},{10,1},{11,2},{12,3},{13,4},{14,5},{15,6},{17,8},{18,9},{19,... | collective-permute-start | bytes 786440 | tf_op jit(solution)/shard_map/ppermute | solution.py:24
  47.8 0.8 copy-start.2
  48.6 0.8 copy-start.3
  49.4 150.1 %collective-permute-start.3 = (bf16[2,512,256]{2,1,0:T(8,128)(2,1)}, bf16[2,512,256]{2,1,0:T(8,128)(2,1)}, u32[]{:S(2)}, u32[]{:S(2)}) collective-permute-start(bf16[2,512,256]{2,1,0:T(8,128)(2,1)} %copy-done.3), channel_id=1, source_target_pairs={{0,1},{1,2},{2,3},{3,4},{4,5},{5,6},{6,7},{8,9},{9,10},{10,11},{11... | collective-permute-start | bytes 1572872 | tf_op jit(solution)/shard_map/ppermute | solution.py:24
  73.7 125.8 %copy-start.4 = (f32[2,512,512]{2,1,0:T(8,128)S(1)}, f32[2,512,512]{2,1,0:T(8,128)}, u32[]{:S(2)}) copy-start(f32[2,512,512]{2,1,0:T(8,128)} %sample.1) | copy-start | bytes 6291460
  73.7 125.8 %collective-permute-start.4 = (bf16[2,256,512]{2,1,0:T(8,128)(2,1)}, bf16[2,256,512]{2,1,0:T(8,128)(2,1)}, u32[]{:S(2)}, u32[]{:S(2)}) collective-permute-start(bf16[2,256,512]{2,1,0:T(8,128)(2,1)} %copy-done.2), channel_id=1, source_target_pairs={{0,8},{1,9},{2,10},{3,11},{4,12},{5,13},{6,14},{7,15},{8,16},{9,17... | collective-permute-start | bytes 1572872 | tf_op jit(solution)/shard_map/ppermute | solution.py:24
  78.9 120.6 %collective-permute-start.5 = (bf16[2,256,256]{2,1,0:T(8,128)(2,1)S(1)}, bf16[2,256,256]{2,1,0:T(8,128)(2,1)}, u32[]{:S(2)}, u32[]{:S(2)}) collective-permute-start(bf16[2,256,256]{2,1,0:T(8,128)(2,1)S(1)} %get-tuple-element.10), channel_id=1, source_target_pairs={{0,9},{1,10},{2,11},{3,12},{4,13},{5,14},{6,15},{8,17},{9,18},{10,... | collective-permute-start | bytes 786440 | tf_op jit(solution)/shard_map/ppermute | solution.py:24
  197.0 2.5 %copy-start.5 = (f32[2,512,512]{2,1,0:T(8,128)S(1)}, f32[2,512,512]{2,1,0:T(8,128)}, u32[]{:S(2)}) copy-start(f32[2,512,512]{2,1,0:T(8,128)} %get-tuple-element.7) | copy-start | bytes 6291460
Sparse Core Ops, SparseCore 0:
  49.6 147.4 all-reduce.4

commit v2 on v1

--- a/solution.py
+++ b/solution.py
@@ -1,3 +1,4 @@
+import functools
 import math
 
 import jax
@@ -195,6 +196,146 @@
             at = slice((j - own) * LANES, (j - own + 1) * LANES)
             right_out[c, :, at] = acc[c, j, :rows, :].astype(bf16)
             corner_out[c, :, at] = acc[c, j, rows:, :].astype(bf16)
+
+
+def exchange_kernel(
+    sample, main, right_grad, below_grad, corner_grad, probe, probe_grad,
+    sample_out, probe_out,
+    from_left, from_above, from_both, parts, col_buf, row_buf, col_sum, row_sum, gathered, whole,
+    halo_send, halo_recv, col_send, col_recv, row_send, row_recv,
+    row_send2, row_recv2, col_send2, col_recv2,
+    *, n_row, n_col, rate,
+):
+    f32, bf16 = jnp.float32, jnp.bfloat16
+    frame = probe.shape[-1]
+    row, col = lax.axis_index("row"), lax.axis_index("col")
+    col_chunk = parts.shape[0] // n_col
+    row_chunk = col_chunk // n_row
+
+    def on_row(k):
+        return (lax.rem(row + k, n_row), col)
+
+    def on_col(k):
+        return (row, lax.rem(col + k, n_col))
+
+    def copy(src, dst, send, recv, to):
+        return pltpu.make_async_remote_copy(
+            src_ref=src, dst_ref=dst, send_sem=send, recv_sem=recv,
+            device_id=to, device_id_type=pl.DeviceIdType.MESH,
+        )
+
+    barrier = pltpu.get_barrier_semaphore()
+    down_right = (lax.rem(row + 1, n_row), lax.rem(col + 1, n_col))
+    up_left = (lax.rem(row + n_row - 1, n_row), lax.rem(col + n_col - 1, n_col))
+    peers = [on_row(k) for k in range(1, n_row)] + [on_col(k) for k in range(1, n_col)]
+    peers += [down_right, up_left]
+    for peer in peers:
+        pl.semaphore_signal(barrier, inc=1, device_id=peer, device_id_type=pl.DeviceIdType.MESH)
+
+    panels = frame // LANES
+    blocks = [(m, c, j) for m in range(2) for c in range(2) for j in range(panels)]
+    for b, (m, c, j) in enumerate(blocks):
+        value = probe_grad[m, c, :, j * LANES : (j + 1) * LANES]
+        parts[b * frame : (b + 1) * frame, :] = value.astype(bf16)
+    pl.semaphore_wait(barrier, len(peers))
+
+    def rows_of(index, size):
+        return pl.ds(pl.multiple_of(index * size, 16), size)
+
+    scatter = [
+        copy(
+            parts.at[rows_of(lax.rem(col + k, n_col), col_chunk)], col_buf.at[k],
+            col_send.at[k], col_recv.at[k], on_col(k),
+        )
+        for k in range(1, n_col)
+    ]
+    for one in scatter:
+        one.start()
+
+    gives_right, gives_below = col < n_col - 1, row < n_row - 1
+    has_left, has_above = col > 0, row > 0
+    halos = [
+        (copy(right_grad, from_left, halo_send.at[0], halo_recv.at[0], on_col(1)),
+         gives_right, has_left),
+        (copy(below_grad, from_above, halo_send.at[1], halo_recv.at[1], on_row(1)),
+         gives_below, has_above),
+        (copy(corner_grad, from_both, halo_send.at[2], halo_recv.at[2], down_right),
+         jnp.logical_and(gives_right, gives_below), jnp.logical_and(has_left, has_above)),
+    ]
+    for one, gives, _ in halos:
+        pl.when(gives)(one.start)
+
+    for one in scatter:
+        one.wait_recv()
+    total = parts[rows_of(col, col_chunk), :].astype(f32)
+    for k in range(1, n_col):
+        total = total + col_buf[k].astype(f32)
+    col_sum[...] = total.astype(bf16)
+    reduce_rows = [
+        copy(
+            col_sum.at[rows_of(lax.rem(row + k, n_row), row_chunk)], row_buf.at[k],
+            row_send.at[k], row_recv.at[k], on_row(k),
+        )
+        for k in range(1, n_row)
+    ]
+    for one in reduce_rows:
+        one.start()
+
+    power = probe[0, 0] ** 2 + probe[0, 1] ** 2 + (probe[1, 0] ** 2 + probe[1, 1] ** 2)
+    scale = 1.0 / (jnp.max(power, keepdims=True) + 1e-06)
+    for c in range(2):
+        sample_out[c] = sample[c] - main[c] * scale
+
+    for one in reduce_rows:
+        one.wait_recv()
+    total = col_sum[rows_of(row, row_chunk), :].astype(f32)
+    for k in range(1, n_row):
+        total = total + row_buf[k].astype(f32)
+    row_sum[...] = total.astype(bf16)
+    gather_rows = [
+        copy(
+            row_sum, gathered.at[rows_of(row, row_chunk)],
+            row_send2.at[k], row_recv2.at[k], on_row(k),
+        )
+        for k in range(1, n_row)
+    ]
+    for one in gather_rows:
+        one.start()
+    gathered[rows_of(row, row_chunk), :] = row_sum[...]
+    for one in gather_rows:
+        one.wait_recv()
+    gather_cols = [
+        copy(
+            gathered, whole.at[rows_of(col, col_chunk)],
+            col_send2.at[k], col_recv2.at[k], on_col(k),
+        )
+        for k in range(1, n_col)
+    ]
+    for one in gather_cols:
+        one.start()
+    whole[rows_of(col, col_chunk), :] = gathered[...]
+
+    def take(one, has, src, rows, cols):
+        @pl.when(has)
+        def _():
+            one.wait_recv()
+            for c in range(2):
+                sample_out[c, :rows, :cols] -= src[c].astype(f32) * scale
+
+    take(halos[0][0], halos[0][2], from_left, *from_left.shape[1:])
+    take(halos[1][0], halos[1][2], from_above, *from_above.shape[1:])
+    take(halos[2][0], halos[2][2], from_both, *from_both.shape[1:])
+
+    for one in gather_cols:
+        one.wait_recv()
+    for b, (m, c, j) in enumerate(blocks):
+        at = slice(j * LANES, (j + 1) * LANES)
+        summed = whole[b * frame : (b + 1) * frame, :].astype(f32)
+        probe_out[m, c, :, at] = probe[m, c, :, at] - rate * summed
+    for one in scatter + reduce_rows + gather_rows + gather_cols:
+        one.wait_send()
+    for one, gives, _ in halos:
+        pl.when(gives)(one.wait_send)
 
 
 def shards(sample, probe_modes, amplitude, offsets, counts):
@@ -235,21 +376,37 @@
         offsets.reshape(-1), counts.reshape(-1), jnp.asarray(tables(frame)), sample,
         right, below, corner, probe_modes, amplitude.reshape(slots, frame, frame),
     )
-    from_left = shifted(right_grad, ("row", "col"), (0, 1))
-    from_above = shifted(below_grad, ("row", "col"), (1, 0))
-    from_both = shifted(corner_grad, ("row", "col"), (1, 1))
-    summed = lax.psum(probe_grad, ("row", "col"))
-
-    def placed(block):
-        tall, broad = rows - block.shape[1], cols - block.shape[2]
-        return jnp.pad(block.astype(f32), ((0, 0), (0, tall), (0, broad)))
-
-    total = main + placed(from_left) + placed(from_above) + placed(from_both)
-    power = jnp.sum(probe_modes[:, 0] ** 2 + probe_modes[:, 1] ** 2, axis=0)
-    new_sample = sample - total / (jnp.max(power) + 1e-06)
-    devices = lax.axis_size("row") * lax.axis_size("col")
-    new_probe = probe_modes - (1.0 / math.sqrt(devices * slots)) * summed
-    return (new_sample, new_probe)
+    n_row, n_col = lax.axis_size("row"), lax.axis_size("col")
+    lines = probe_modes.size // LANES
+    col_chunk = lines // n_col
+    row_chunk = col_chunk // n_row
+    dma = pltpu.SemaphoreType.DMA
+    return pl.pallas_call(
+        functools.partial(
+            exchange_kernel, n_row=n_row, n_col=n_col, rate=1.0 / math.sqrt(n_row * n_col * slots)
+        ),
+        out_shape=(shape(sample.shape, f32), shape(probe_modes.shape, f32)),
+        in_specs=[vmem] * 7,
+        out_specs=(vmem,) * 2,
+        scratch_shapes=[
+            pltpu.VMEM((2, rows, frame), bf16),
+            pltpu.VMEM((2, frame, cols), bf16),
+            pltpu.VMEM((2, frame, frame), bf16),
+            pltpu.VMEM((lines, LANES), bf16),
+            pltpu.VMEM((n_col, col_chunk, LANES), bf16),
+            pltpu.VMEM((n_row, row_chunk, LANES), bf16),
+            pltpu.VMEM((col_chunk, LANES), bf16),
+            pltpu.VMEM((row_chunk, LANES), bf16),
+            pltpu.VMEM((col_chunk, LANES), bf16),
+            pltpu.VMEM((lines, LANES), bf16),
+            dma((3,)), dma((3,)),
+            dma((n_col,)), dma((n_col,)), dma((n_row,)), dma((n_row,)),
+            dma((n_row,)), dma((n_row,)), dma((n_col,)), dma((n_col,)),
+        ],
+        compiler_params=pltpu.CompilerParams(
+            collective_id=0, has_side_effects=True, vmem_limit_bytes=48 * 1024 * 1024
+        ),
+    )(sample, main, right_grad, below_grad, corner_grad, probe_modes, probe_grad)
 
 
 def solution(mesh):

time: 211 us -> 100 us (0.47); the launches traced: 210 us -> 102 us
  waiting for transfers between devices: 133 us -> 17.3 us
  Pallas kernels: 15.1 us -> 71.6 us
  starting transfers between devices: 32.4 us -> 3.85 us
  between operations: 15.4 us -> 1.37 us
  other arithmetic: 9.82 us -> 1.73 us
  local copies, waits for them, and re-layouts: 3.49 us -> 5.91 us
    psum x1 -> x0, waiting for transfers between devices: 116 us -> none  [shards(): summed = lax.psum(probe_grad, ('row', 'col'))]
    pallas_call x0 -> x1, Pallas kernels: none -> 58.1 us  [shards(): pl.pallas_call(functools.partial(exchange_kernel, n_row=n_row, n_col=n_co...]
    ppermute x6 -> x3, starting transfers between devices: 32.4 us -> 3.85 us  [shifted(): return lax.ppermute(block, axes, route)]
    sub x2 -> x0, other arithmetic: 5.71 us -> none  [the longest x1 3.23 us: shards(): new_sample = sample - total / (jnp.max(power) + 1e-06)]
    unnamed x15 -> x9, local copies, waits for them, and re-layouts: 1.73 us -> 4.15 us
    ppermute x6 -> x3, waiting for transfers between devices: 17.3 us -> 17.3 us  [shifted(): return lax.ppermute(block, axes, route)]
  transfers between devices with their start and end apart: 7 -> 3, of which waited for: 2 -> 1; matrix products, arithmetic and copies ran while one was open for 3% -> 1% of each run, Pallas kernels for 0% -> 0%
where the time goes in v2:
time: 100 us; the launch traced here: 102 us
  Pallas kernels  71.6 us (72%)
  waiting for transfers between devices  17.3 us (17%)
  local copies, waits for them, and re-layouts  5.91 us (6%)
  starting transfers between devices  3.85 us (4%)
  other arithmetic  1.73 us (2%)
  between operations  1.37 us (1%)
    pallas_call x1, Pallas kernels, shards(): pl.pallas_call(functools.partial(exchange_kernel, n_row=n_row, n_col=n_co...  58.1 us
    ppermute x3, waiting for transfers between devices, shifted(): return lax.ppermute(block, axes, route)  17.3 us
    pallas_call x1, Pallas kernels, shards(): pl.pallas_call(gradient_kernel, out_shape=(shape((2, rows, cols), f32), s...  13.5 us
    unnamed x9, local copies, waits for them, and re-layouts  4.15 us
    ppermute x3, starting transfers between devices, shifted(): return lax.ppermute(block, axes, route)  3.85 us
  transfers between devices with their start and end apart: 3, of which 1 were waited for; matrix products, arithmetic and copies ran while one was open for 1% of the time, Pallas kernels for 0%

profile of v2, /device:TPU:0, one launch (start us, length us, event | category | flops | bytes accessed | tf_op | source)
XLA Modules:
  0.0 101.7 jit_solution(3698383368316916078)
XLA Ops:
  0.6 1.7 %convert_element_type.3 = bf16[2,512,512]{2,1,0:T(8,128)(2,1)S(1)} convert(f32[2,512,512]{2,1,0:T(8,128)} %sample.3) | non-fusion elementwise | flops 524288 | bytes 3145728 | tf_op jit(solution)/shard_map/convert_element_type | solution.py:346
  2.4 0.0 copy-start.2
  2.4 0.0 copy-start
  2.4 0.0 copy-start.1
  2.4 0.8 slice.12
  3.2 1.3 %collective-permute-start = (bf16[2,512,256]{2,1,0:T(8,128)(2,1)}, bf16[2,512,256]{2,1,0:T(8,128)(2,1)S(1)}, u32[]{:S(2)}, u32[]{:S(2)}) collective-permute-start(bf16[2,512,256]{2,1,0:T(8,128)(2,1)} %slice.12), channel_id=1, source_target_pairs={{1,0},{2,1},{3,2},{4,3},{5,4},{6,5},{7,6},{9,8},{10,9},{11,10},{12... | collective-permute-start | bytes 1572872 | tf_op jit(solution)/shard_map/ppermute | solution.py:25
  4.5 0.8 slice.13
  5.3 1.3 %collective-permute-start.1 = (bf16[2,256,512]{2,1,0:T(8,128)(2,1)}, bf16[2,256,512]{2,1,0:T(8,128)(2,1)S(1)}, u32[]{:S(2)}, u32[]{:S(2)}) collective-permute-start(bf16[2,256,512]{2,1,0:T(8,128)(2,1)} %slice.13), channel_id=1, source_target_pairs={{8,0},{9,1},{10,2},{11,3},{12,4},{13,5},{14,6},{15,7},{16,8},{17,9... | collective-permute-start | bytes 1572872 | tf_op jit(solution)/shard_map/ppermute | solution.py:25
  6.7 1.3 %collective-permute-start.2 = (bf16[2,256,256]{2,1,0:T(8,128)(2,1)S(1)}, bf16[2,256,256]{2,1,0:T(8,128)(2,1)S(1)}, u32[]{:S(2)}, u32[]{:S(2)}) collective-permute-start(bf16[2,256,256]{2,1,0:T(8,128)(2,1)S(1)} %slice.14), channel_id=1, source_target_pairs={{9,0},{10,1},{11,2},{12,3},{13,4},{14,5},{15,6},{17,8},{18,9},{19,... | collective-permute-start | bytes 786440 | tf_op jit(solution)/shard_map/ppermute | solution.py:25
  8.6 0.0 copy-done.2
  8.6 0.1 copy.9
  8.7 0.1 reshape.13.offsets
  8.8 17.3 %collective-permute-done.2.corner = bf16[2,256,256]{2,1,0:T(8,128)(2,1)S(1)} collective-permute-done((bf16[2,256,256]{2,1,0:T(8,128)(2,1)S(1)}, bf16[2,256,256]{2,1,0:T(8,128)(2,1)S(1)}, u32[]{:S(2)}, u32[]{:S(2)}) %collective-permute-start.2) | collective-permute-done | bytes 262176 | tf_op jit(solution)/shard_map/ppermute | solution.py:25
  26.1 0.0 collective-permute-done.right
  26.1 0.0 collective-permute-done.1.below
  26.1 0.0 copy-done
  26.1 0.0 copy-done.1
  26.1 13.5 %shard_map.77 = (f32[2,512,512]{2,1,0:T(8,128)}, bf16[2,512,256]{2,1,0:T(8,128)(2,1)S(1)}, bf16[2,256,512]{2,1,0:T(8,128)(2,1)S(1)}, bf16[2,256,256]{2,1,0:T(8,128)(2,1)S(1)}, f32[2,2,256,256]{3,2,1,0:T(8,128)S(1)}) custom-call(s32[32]{0:T(128)S(1)} %reshape.13.offsets, s32[1]{0:T(128)} %bitcast.4.counts, bf16[6,256,256]{2,1,0:T(8,128)(2,1)S(1)} %copy-done.1, ...), custom_call_target="tpu_custom_call" | custom-call | tf_op jit(solution)/shard_map/pallas_call | solution.py:354
  39.5 58.1 %shard_map.78 = (f32[2,512,512]{2,1,0:T(8,128)}, f32[2,2,256,256]{3,2,1,0:T(8,128)S(1)}) custom-call(f32[2,512,512]{2,1,0:T(8,128)} %sample.3, f32[2,512,512]{2,1,0:T(8,128)} %get-tuple-element.7.main, bf16[2,512,256]{2,1,0:T(8,128)(2,1)S(1)} %get-tuple-element.8.right_grad, bf16[2,256,512]{2,1,0:T(8,128)(2,1)S(1)} %get-tuple-element.9.below_grad, ...), custom_call_target="tpu_custom_call" | custom-call | tf_op jit(solution)/shard_map/pallas_call | solution.py:384
  97.6 3.1 %copy.13 = f32[2,512,512]{2,1,0:T(8,128)} copy(f32[2,512,512]{2,1,0:T(8,128)} %get-tuple-element.14) | data formatting | bytes 4194304
  100.7 1.0 copy.14
  (1 shorter events, 0.0 us)
Async XLA Ops:
  2.4 6.2 %copy-start.2 = (s32[1,1,16,2]{2,3,1,0:T(2,128)S(1)}, s32[1,1,16,2]{2,3,1,0:T(2,128)}, u32[]{:S(2)}) copy-start(s32[1,1,16,2]{2,3,1,0:T(2,128)} %param.9) | copy-start | bytes 388
  2.4 23.7 %copy-start = (f32[2,2,256,256]{3,2,1,0:T(8,128)S(1)}, f32[2,2,256,256]{3,2,1,0:T(8,128)}, u32[]{:S(2)}) copy-start(f32[2,2,256,256]{3,2,1,0:T(8,128)} %probe.3) | copy-start | bytes 3145732
  2.4 23.7 %copy-start.1 = (bf16[6,256,256]{2,1,0:T(8,128)(2,1)S(1)}, bf16[6,256,256]{2,1,0:T(8,128)(2,1)}, u32[]{:S(2)}) copy-start(bf16[6,256,256]{2,1,0:T(8,128)(2,1)} %constant.2.clone.table) | copy-start | bytes 2359300
  3.2 22.8 %collective-permute-start = (bf16[2,512,256]{2,1,0:T(8,128)(2,1)}, bf16[2,512,256]{2,1,0:T(8,128)(2,1)S(1)}, u32[]{:S(2)}, u32[]{:S(2)}) collective-permute-start(bf16[2,512,256]{2,1,0:T(8,128)(2,1)} %slice.12), channel_id=1, source_target_pairs={{1,0},{2,1},{3,2},{4,3},{5,4},{6,5},{7,6},{9,8},{10,9},{11,10},{12... | collective-permute-start | bytes 1572872 | tf_op jit(solution)/shard_map/ppermute | solution.py:25
  5.3 20.7 %collective-permute-start.1 = (bf16[2,256,512]{2,1,0:T(8,128)(2,1)}, bf16[2,256,512]{2,1,0:T(8,128)(2,1)S(1)}, u32[]{:S(2)}, u32[]{:S(2)}) collective-permute-start(bf16[2,256,512]{2,1,0:T(8,128)(2,1)} %slice.13), channel_id=1, source_target_pairs={{8,0},{9,1},{10,2},{11,3},{12,4},{13,5},{14,6},{15,7},{16,8},{17,9... | collective-permute-start | bytes 1572872 | tf_op jit(solution)/shard_map/ppermute | solution.py:25
  6.7 19.4 %collective-permute-start.2 = (bf16[2,256,256]{2,1,0:T(8,128)(2,1)S(1)}, bf16[2,256,256]{2,1,0:T(8,128)(2,1)S(1)}, u32[]{:S(2)}, u32[]{:S(2)}) collective-permute-start(bf16[2,256,256]{2,1,0:T(8,128)(2,1)S(1)} %slice.14), channel_id=1, source_target_pairs={{9,0},{10,1},{11,2},{12,3},{13,4},{14,5},{15,6},{17,8},{18,9},{19,... | collective-permute-start | bytes 786440 | tf_op jit(solution)/shard_map/ppermute | solution.py:25

commit v3 on v2

--- a/solution.py
+++ b/solution.py
@@ -14,17 +14,6 @@
 CHUNK = 16
 
 
-def shifted(block, axes, distances):
-    sizes = [lax.axis_size(a) for a in axes]
-    route = []
-    for flat in range(math.prod(sizes)):
-        at = np.unravel_index(flat, sizes)
-        to = [int(i) + d for i, d in zip(at, distances)]
-        if all(0 <= i < n for i, n in zip(to, sizes)):
-            route.append((flat, int(np.ravel_multi_index(to, sizes))))
-    return lax.ppermute(block, axes, route)
-
-
 def tables(frame):
     index = np.arange(frame)
     angle = 2.0 * math.pi / frame * ((index[:, None] * index[None, :]) % frame)
@@ -40,6 +29,62 @@
     pick = np.eye(frame)[order]
     stack = np.stack([even, odd, even.T, odd.T, pick, pick.T])
     return stack.astype(np.float32).astype(ml_dtypes.bfloat16)
+
+
+def halo_kernel(
+    sample, right_out, below_out, corner_out,
+    right_in, below_in, corner_in, edge, edge_below, edge_corner, send, recv,
+    *, n_row, n_col,
+):
+    bf16 = jnp.bfloat16
+    frame = right_out.shape[-1]
+    row, col = lax.axis_index("row"), lax.axis_index("col")
+    left = (row, lax.rem(col + n_col - 1, n_col))
+    right = (row, lax.rem(col + 1, n_col))
+    up = (lax.rem(row + n_row - 1, n_row), col)
+    down = (lax.rem(row + 1, n_row), col)
+    up_left = (up[0], left[1])
+    down_right = (down[0], right[1])
+    barrier = pltpu.get_barrier_semaphore()
+    peers = (left, right, up, down, up_left, down_right)
+    for peer in peers:
+        pl.semaphore_signal(barrier, inc=1, device_id=peer, device_id_type=pl.DeviceIdType.MESH)
+    edge[...] = sample[:, :, :frame].astype(bf16)
+    edge_below[...] = sample[:, :frame, :].astype(bf16)
+    edge_corner[...] = sample[:, :frame, :frame].astype(bf16)
+    pl.semaphore_wait(barrier, len(peers))
+    to_left, to_up = col > 0, row > 0
+    has_right, has_below = col < n_col - 1, row < n_row - 1
+    plan = [
+        (edge, right_in, left, to_left, has_right, right_out),
+        (edge_below, below_in, up, to_up, has_below, below_out),
+        (edge_corner, corner_in, up_left, jnp.logical_and(to_left, to_up),
+         jnp.logical_and(has_right, has_below), corner_out),
+    ]
+    copies = [
+        pltpu.make_async_remote_copy(
+            src_ref=src, dst_ref=dst, send_sem=send.at[i], recv_sem=recv.at[i],
+            device_id=to, device_id_type=pl.DeviceIdType.MESH,
+        )
+        for i, (src, dst, to, _, _, _) in enumerate(plan)
+    ]
+    for one, item in zip(copies, plan):
+        pl.when(item[3])(one.start)
+
+    def finish(one, dst, has, out):
+        @pl.when(has)
+        def _():
+            one.wait_recv()
+            out[...] = dst[...]
+
+        @pl.when(jnp.logical_not(has))
+        def _():
+            out[...] = jnp.zeros_like(out)
+
+    for one, item in zip(copies, plan):
+        finish(one, item[1], item[4], item[5])
+    for one, item in zip(copies, plan):
+        pl.when(item[3])(one.wait_send)
 
 
 def gradient_kernel(
@@ -270,7 +315,7 @@
     total = parts[rows_of(col, col_chunk), :].astype(f32)
     for k in range(1, n_col):
         total = total + col_buf[k].astype(f32)
-    col_sum[...] = total.astype(bf16)
+    col_sum[...] = total
     reduce_rows = [
         copy(
             col_sum.at[rows_of(lax.rem(row + k, n_row), row_chunk)], row_buf.at[k],
@@ -288,9 +333,9 @@
 
     for one in reduce_rows:
         one.wait_recv()
-    total = col_sum[rows_of(row, row_chunk), :].astype(f32)
+    total = col_sum[rows_of(row, row_chunk), :]
     for k in range(1, n_row):
-        total = total + row_buf[k].astype(f32)
+        total = total + row_buf[k]
     row_sum[...] = total.astype(bf16)
     gather_rows = [
         copy(
@@ -343,14 +388,23 @@
     rows, cols = sample.shape[1:]
     slots = amplitude.shape[2]
     f32, bf16 = jnp.float32, jnp.bfloat16
-    edge = sample.astype(bf16)
-    right = shifted(edge[:, :, :frame], ("row", "col"), (0, -1))
-    below = shifted(edge[:, :frame, :], ("row", "col"), (-1, 0))
-    corner = shifted(edge[:, :frame, :frame], ("row", "col"), (-1, -1))
     panels = (cols + frame) // LANES
     shape = jax.ShapeDtypeStruct
     vmem = pl.BlockSpec(memory_space=pltpu.VMEM)
     smem = pl.BlockSpec(memory_space=pltpu.SMEM)
+    n_row, n_col = lax.axis_size("row"), lax.axis_size("col")
+    dma = pltpu.SemaphoreType.DMA
+    halo_shapes = ((2, rows, frame), (2, frame, cols), (2, frame, frame))
+    right, below, corner = pl.pallas_call(
+        functools.partial(halo_kernel, n_row=n_row, n_col=n_col),
+        out_shape=tuple(shape(h, bf16) for h in halo_shapes),
+        in_specs=[vmem],
+        out_specs=(vmem,) * 3,
+        scratch_shapes=[pltpu.VMEM(h, bf16) for h in halo_shapes * 2] + [dma((3,)), dma((3,))],
+        compiler_params=pltpu.CompilerParams(
+            collective_id=1, has_side_effects=True, vmem_limit_bytes=32 * 1024 * 1024
+        ),
+    )(sample)
     main, right_grad, below_grad, corner_grad, probe_grad = pl.pallas_call(
         gradient_kernel,
         out_shape=(
@@ -376,11 +430,9 @@
         offsets.reshape(-1), counts.reshape(-1), jnp.asarray(tables(frame)), sample,
         right, below, corner, probe_modes, amplitude.reshape(slots, frame, frame),
     )
-    n_row, n_col = lax.axis_size("row"), lax.axis_size("col")
     lines = probe_modes.size // LANES
     col_chunk = lines // n_col
     row_chunk = col_chunk // n_row
-    dma = pltpu.SemaphoreType.DMA
     return pl.pallas_call(
         functools.partial(
             exchange_kernel, n_row=n_row, n_col=n_col, rate=1.0 / math.sqrt(n_row * n_col * slots)
@@ -394,8 +446,8 @@
             pltpu.VMEM((2, frame, frame), bf16),
             pltpu.VMEM((lines, LANES), bf16),
             pltpu.VMEM((n_col, col_chunk, LANES), bf16),
-            pltpu.VMEM((n_row, row_chunk, LANES), bf16),
-            pltpu.VMEM((col_chunk, LANES), bf16),
+            pltpu.VMEM((n_row, row_chunk, LANES), f32),
+            pltpu.VMEM((col_chunk, LANES), f32),
             pltpu.VMEM((row_chunk, LANES), bf16),
             pltpu.VMEM((col_chunk, LANES), bf16),
             pltpu.VMEM((lines, LANES), bf16),

time: 100 us -> 99.9 us (level); the launches traced: 102 us -> 99.1 us
  Pallas kernels: 71.6 us -> 91.3 us
  waiting for transfers between devices: 17.3 us -> 0 us
  starting transfers between devices: 3.85 us -> 0 us
  other arithmetic: 1.73 us -> 0 us
    pallas_call x0 -> x1, Pallas kernels: none -> 20.6 us  [shards(): pl.pallas_call(functools.partial(halo_kernel, n_row=n_row, n_col=n_col),...]
    ppermute x3 -> x0, waiting for transfers between devices: 17.3 us -> none  [shifted(): return lax.ppermute(block, axes, route)]
    pallas_call x1, Pallas kernels: 13.5 us -> 8.14 us  [shards(): pl.pallas_call(gradient_kernel, out_shape=(shape((2, rows, cols), f32), s...]
    pallas_call x1, Pallas kernels: 58.1 us -> 62.5 us  [shards(): pl.pallas_call(functools.partial(exchange_kernel, n_row=n_row, n_col=n_co...]
    ppermute x3 -> x0, starting transfers between devices: 3.85 us -> none  [shifted(): return lax.ppermute(block, axes, route)]
    unnamed x9, local copies, waits for them, and re-layouts: 4.15 us -> 6.4 us
    convert_element_type x1 -> x0, other arithmetic: 1.73 us -> none  [shards(): edge = sample.astype(bf16)]
    slice x3 -> x0, local copies, waits for them, and re-layouts: 1.67 us -> none  [the longest x1 0.83 us: shards(): right = shifted(edge[:, :, :frame], ('row', 'col'), (0, -1))]
  transfers between devices with their start and end apart: 3 -> 0, of which waited for: 1 -> 0; matrix products, arithmetic and copies ran while one was open for 1% -> 0% of each run, Pallas kernels for 0% -> 0%
where the time goes in v3:
time: 99.9 us; the launch traced here: 99.1 us
  Pallas kernels  91.3 us (91%)
  local copies, waits for them, and re-layouts  6.49 us (6%)
  between operations  1.32 us (1%)
    pallas_call x1, Pallas kernels, shards(): pl.pallas_call(functools.partial(exchange_kernel, n_row=n_row, n_col=n_co...  62.5 us
    pallas_call x1, Pallas kernels, shards(): pl.pallas_call(functools.partial(halo_kernel, n_row=n_row, n_col=n_col),...  20.6 us
    pallas_call x1, Pallas kernels, shards(): pl.pallas_call(gradient_kernel, out_shape=(shape((2, rows, cols), f32), s...  8.14 us
    unnamed x9, local copies, waits for them, and re-layouts  6.4 us

profile of v3, /device:TPU:0, one launch (start us, length us, event | category | flops | bytes accessed | tf_op | source)
XLA Modules:
  0.0 99.1 jit_solution(2231822269677866056)
XLA Ops:
  1.3 0.8 copy.9
  2.0 0.1 reshape.13.offsets
  2.1 0.0 copy-start
  2.1 1.6 %copy-done = f32[2,512,512]{2,1,0:T(8,128)S(1)} copy-done((f32[2,512,512]{2,1,0:T(8,128)S(1)}, f32[2,512,512]{2,1,0:T(8,128)}, u32[]{:S(2)}) %copy-start) | copy-done | bytes 2097176
  3.7 0.0 copy-start.1
  3.7 0.0 copy-start.2
  3.7 20.6 %shard_map.77 = (bf16[2,512,256]{2,1,0:T(8,128)(2,1)S(1)}, bf16[2,256,512]{2,1,0:T(8,128)(2,1)S(1)}, bf16[2,256,256]{2,1,0:T(8,128)(2,1)S(1)}) custom-call(f32[2,512,512]{2,1,0:T(8,128)S(1)} %copy-done), custom_call_target="tpu_custom_call" | custom-call | tf_op jit(solution)/shard_map/pallas_call | solution.py:398
  24.3 0.0 copy-done.1
  24.3 0.0 copy-done.2
  24.3 8.1 %shard_map.78 = (f32[2,512,512]{2,1,0:T(8,128)}, bf16[2,512,256]{2,1,0:T(8,128)(2,1)S(1)}, bf16[2,256,512]{2,1,0:T(8,128)(2,1)S(1)}, bf16[2,256,256]{2,1,0:T(8,128)(2,1)S(1)}, f32[2,2,256,256]{3,2,1,0:T(8,128)S(1)}) custom-call(s32[32]{0:T(128)S(1)} %reshape.13.offsets, s32[1]{0:T(128)} %bitcast.4.counts, bf16[6,256,256]{2,1,0:T(8,128)(2,1)S(1)} %copy-done.2, ...), custom_call_target="tpu_custom_call" | custom-call | tf_op jit(solution)/shard_map/pallas_call | solution.py:408
  32.5 62.5 %shard_map.79 = (f32[2,512,512]{2,1,0:T(8,128)}, f32[2,2,256,256]{3,2,1,0:T(8,128)S(1)}) custom-call(f32[2,512,512]{2,1,0:T(8,128)} %sample.5, f32[2,512,512]{2,1,0:T(8,128)} %get-tuple-element.13.main, bf16[2,512,256]{2,1,0:T(8,128)(2,1)S(1)} %get-tuple-element.14.right_grad, bf16[2,256,512]{2,1,0:T(8,128)(2,1)S(1)} %get-tuple-element.15.below_grad, ...), custom_call_target="tpu_custom_call" | custom-call | tf_op jit(solution)/shard_map/pallas_call | solution.py:436
  95.0 3.1 %copy.13 = f32[2,512,512]{2,1,0:T(8,128)} copy(f32[2,512,512]{2,1,0:T(8,128)} %get-tuple-element.20) | data formatting | bytes 4194304
  98.1 1.0 copy.14
Async XLA Ops:
  2.1 1.6 %copy-start = (f32[2,512,512]{2,1,0:T(8,128)S(1)}, f32[2,512,512]{2,1,0:T(8,128)}, u32[]{:S(2)}) copy-start(f32[2,512,512]{2,1,0:T(8,128)} %sample.5) | copy-start | bytes 6291460
  3.7 20.6 %copy-start.1 = (f32[2,2,256,256]{3,2,1,0:T(8,128)S(1)}, f32[2,2,256,256]{3,2,1,0:T(8,128)}, u32[]{:S(2)}) copy-start(f32[2,2,256,256]{3,2,1,0:T(8,128)} %probe.3) | copy-start | bytes 3145732
  3.7 20.6 %copy-start.2 = (bf16[6,256,256]{2,1,0:T(8,128)(2,1)S(1)}, bf16[6,256,256]{2,1,0:T(8,128)(2,1)}, u32[]{:S(2)}) copy-start(bf16[6,256,256]{2,1,0:T(8,128)(2,1)} %constant.2.clone.table) | copy-start | bytes 2359300

commit v4 on v3

--- a/solution.py
+++ b/solution.py
@@ -90,7 +90,7 @@
 def gradient_kernel(
     offsets, counts, table, sample, right, below, corner, probe, amplitude,
     main_out, right_out, below_out, corner_out, probe_out,
-    ext, acc, patch, xs, ys, zs, gs,
+    ext, acc, *pairs,
 ):
     rows, cols = sample.shape[1:]
     frame = probe.shape[-1]
@@ -114,7 +114,8 @@
     def dot(a, b):
         return jnp.dot(a, b, preferred_element_type=f32)
 
-    def visit(slot, carry):
+    def visit(slot, turn):
+        patch, xs, ys, zs, gs = (ref.at[turn] for ref in pairs)
         row_at = offsets[2 * slot]
         col_at = offsets[2 * slot + 1]
         panel = col_at // LANES
@@ -159,6 +160,7 @@
                         xs[0, to, at] = (low + high).astype(bf16)
                         xs[1, to, at] = (low - high).astype(bf16)
 
+        yield
         for p in range(2):
             product = dot(table[p], xs[p])
             for m in range(2):
@@ -170,6 +172,7 @@
                     ys[0, to, at] = (low + high).astype(bf16)
                     ys[1, to, at] = (low - high).astype(bf16)
 
+        yield
         for q in range(2):
             far = dot(ys[q], table[2 + q])
             for p in range(2):
@@ -183,6 +186,7 @@
                     for c in range(2):
                         zs[p, c * half : (c + 1) * half, at] = (fields[m][c] * factor).astype(bf16)
 
+        yield
         from_even = dot(table[2], zs[0])
         from_odd = dot(table[3], zs[1])
         for h, back in enumerate((from_even + from_odd, from_even - from_odd)):
@@ -195,6 +199,7 @@
                             c * half : (c + 1) * half, at
                         ].astype(bf16)
 
+        yield
         grad_even = dot(gs[0], table[0])
         grad_odd = dot(gs[1], table[1])
         for t in range(0, frame, CHUNK):
@@ -228,9 +233,24 @@
                 )
                 for j in range(3):
                     acc[c, panel + j, pl.ds(row_at + t, CHUNK), :] += spread[j]
+        yield
+
+    def both(pair, carry):
+        first, second = visit(2 * pair, 0), visit(2 * pair + 1, 1)
+        next(first)
+        for _ in range(4):
+            next(first)
+            next(second)
+        next(second)
         return carry
 
-    lax.fori_loop(0, counts[0], visit, 0)
+    live = counts[0]
+    lax.fori_loop(0, live // 2, both, 0)
+
+    @pl.when(live % 2 == 1)
+    def _():
+        for _ in visit(live - 1, 0):
+            pass
 
     for c in range(2):
         for j in range(own):
@@ -419,11 +439,11 @@
         scratch_shapes=[
             pltpu.VMEM((2, panels, rows + frame, LANES), f32),
             pltpu.VMEM((2, panels, rows + frame, LANES), f32),
-            pltpu.VMEM((2, frame, frame), f32),
-            pltpu.VMEM((2, frame, 2 * frame), bf16),
-            pltpu.VMEM((2, 2 * frame, frame), bf16),
-            pltpu.VMEM((2, frame, 2 * frame), bf16),
-            pltpu.VMEM((2, 2 * frame, frame), bf16),
+            pltpu.VMEM((2, 2, frame, frame), f32),
+            pltpu.VMEM((2, 2, frame, 2 * frame), bf16),
+            pltpu.VMEM((2, 2, 2 * frame, frame), bf16),
+            pltpu.VMEM((2, 2, frame, 2 * frame), bf16),
+            pltpu.VMEM((2, 2, 2 * frame, frame), bf16),
         ],
         compiler_params=pltpu.CompilerParams(vmem_limit_bytes=48 * 1024 * 1024),
     )(

time: 99.9 us -> 93.6 us (0.937)
  Pallas kernels: 91.3 us -> 85.2 us
    pallas_call x1, Pallas kernels: 62.5 us -> 50.1 us  [shards(): pl.pallas_call(functools.partial(exchange_kernel, n_row=n_row, n_col=n_co...]
    pallas_call x1, Pallas kernels: 8.14 us -> 14.6 us  [shards(): pl.pallas_call(gradient_kernel, out_shape=(shape((2, rows, cols), f32), s...]
where the time goes in v4:
time: 93.6 us; the launch traced here: 93 us
  Pallas kernels  85.2 us (91%)
  local copies, waits for them, and re-layouts  6.49 us (7%)
  between operations  1.32 us (1%)
    pallas_call x1, Pallas kernels, shards(): pl.pallas_call(functools.partial(exchange_kernel, n_row=n_row, n_col=n_co...  50.1 us
    pallas_call x1, Pallas kernels, shards(): pl.pallas_call(functools.partial(halo_kernel, n_row=n_row, n_col=n_col),...  20.6 us
    pallas_call x1, Pallas kernels, shards(): pl.pallas_call(gradient_kernel, out_shape=(shape((2, rows, cols), f32), s...  14.6 us
    unnamed x9, local copies, waits for them, and re-layouts  6.4 us

profile of v4, /device:TPU:0, one launch (start us, length us, event | category | flops | bytes accessed | tf_op | source)
XLA Modules:
  0.0 93.0 jit_solution(1917174463027909565)
XLA Ops:
  1.3 0.8 copy.9
  2.0 0.1 reshape.13.offsets
  2.1 0.0 copy-start
  2.1 1.6 %copy-done = f32[2,512,512]{2,1,0:T(8,128)S(1)} copy-done((f32[2,512,512]{2,1,0:T(8,128)S(1)}, f32[2,512,512]{2,1,0:T(8,128)}, u32[]{:S(2)}) %copy-start) | copy-done | bytes 2097176
  3.7 0.0 copy-start.1
  3.7 0.0 copy-start.2
  3.7 20.6 %shard_map.77 = (bf16[2,512,256]{2,1,0:T(8,128)(2,1)S(1)}, bf16[2,256,512]{2,1,0:T(8,128)(2,1)S(1)}, bf16[2,256,256]{2,1,0:T(8,128)(2,1)S(1)}) custom-call(f32[2,512,512]{2,1,0:T(8,128)S(1)} %copy-done), custom_call_target="tpu_custom_call" | custom-call | tf_op jit(solution)/shard_map/pallas_call | solution.py:418
  24.3 0.0 copy-done.1
  24.3 0.0 copy-done.2
  24.3 14.6 %shard_map.78 = (f32[2,512,512]{2,1,0:T(8,128)}, bf16[2,512,256]{2,1,0:T(8,128)(2,1)S(1)}, bf16[2,256,512]{2,1,0:T(8,128)(2,1)S(1)}, bf16[2,256,256]{2,1,0:T(8,128)(2,1)S(1)}, f32[2,2,256,256]{3,2,1,0:T(8,128)S(1)}) custom-call(s32[32]{0:T(128)S(1)} %reshape.13.offsets, s32[1]{0:T(128)} %bitcast.4.counts, bf16[6,256,256]{2,1,0:T(8,128)(2,1)S(1)} %copy-done.2, ...), custom_call_target="tpu_custom_call" | custom-call | tf_op jit(solution)/shard_map/pallas_call | solution.py:428
  38.9 50.1 %shard_map.79 = (f32[2,512,512]{2,1,0:T(8,128)}, f32[2,2,256,256]{3,2,1,0:T(8,128)S(1)}) custom-call(f32[2,512,512]{2,1,0:T(8,128)} %sample.5, f32[2,512,512]{2,1,0:T(8,128)} %get-tuple-element.13.main, bf16[2,512,256]{2,1,0:T(8,128)(2,1)S(1)} %get-tuple-element.14.right_grad, bf16[2,256,512]{2,1,0:T(8,128)(2,1)S(1)} %get-tuple-element.15.below_grad, ...), custom_call_target="tpu_custom_call" | custom-call | tf_op jit(solution)/shard_map/pallas_call | solution.py:456
  89.0 3.1 %copy.13 = f32[2,512,512]{2,1,0:T(8,128)} copy(f32[2,512,512]{2,1,0:T(8,128)} %get-tuple-element.20) | data formatting | bytes 4194304
  92.1 1.0 %copy.14 = f32[2,2,256,256]{3,2,1,0:T(8,128)} copy(f32[2,2,256,256]{3,2,1,0:T(8,128)S(1)} %get-tuple-element.21) | data formatting | bytes 2097152
Async XLA Ops:
  2.1 1.6 %copy-start = (f32[2,512,512]{2,1,0:T(8,128)S(1)}, f32[2,512,512]{2,1,0:T(8,128)}, u32[]{:S(2)}) copy-start(f32[2,512,512]{2,1,0:T(8,128)} %sample.5) | copy-start | bytes 6291460
  3.7 20.6 %copy-start.1 = (f32[2,2,256,256]{3,2,1,0:T(8,128)S(1)}, f32[2,2,256,256]{3,2,1,0:T(8,128)}, u32[]{:S(2)}) copy-start(f32[2,2,256,256]{3,2,1,0:T(8,128)} %probe.3) | copy-start | bytes 3145732
  3.7 20.6 %copy-start.2 = (bf16[6,256,256]{2,1,0:T(8,128)(2,1)S(1)}, bf16[6,256,256]{2,1,0:T(8,128)(2,1)}, u32[]{:S(2)}) copy-start(bf16[6,256,256]{2,1,0:T(8,128)(2,1)} %constant.2.clone.table) | copy-start | bytes 2359300

commit v5 on v4

--- a/solution.py
+++ b/solution.py
@@ -322,13 +322,14 @@
     halos = [
         (copy(right_grad, from_left, halo_send.at[0], halo_recv.at[0], on_col(1)),
          gives_right, has_left),
-        (copy(below_grad, from_above, halo_send.at[1], halo_recv.at[1], on_row(1)),
+        (copy(below_grad.at[0], from_above.at[0], halo_send.at[1], halo_recv.at[1], on_row(1)),
+         gives_below, has_above),
+        (copy(below_grad.at[1], from_above.at[1], halo_send.at[3], halo_recv.at[3], on_row(1)),
          gives_below, has_above),
         (copy(corner_grad, from_both, halo_send.at[2], halo_recv.at[2], down_right),
          jnp.logical_and(gives_right, gives_below), jnp.logical_and(has_left, has_above)),
     ]
-    for one, gives, _ in halos:
-        pl.when(gives)(one.start)
+    pl.when(halos[1][1])(halos[1][0].start)
 
     for one in scatter:
         one.wait_recv()
@@ -345,6 +346,7 @@
     ]
     for one in reduce_rows:
         one.start()
+    pl.when(halos[0][1])(halos[0][0].start)
 
     power = probe[0, 0] ** 2 + probe[0, 1] ** 2 + (probe[1, 0] ** 2 + probe[1, 1] ** 2)
     scale = 1.0 / (jnp.max(power, keepdims=True) + 1e-06)
@@ -369,6 +371,8 @@
     gathered[rows_of(row, row_chunk), :] = row_sum[...]
     for one in gather_rows:
         one.wait_recv()
+    for one, gives, _ in halos[2:]:
+        pl.when(gives)(one.start)
     gather_cols = [
         copy(
             gathered, whole.at[rows_of(col, col_chunk)],
@@ -380,16 +384,20 @@
         one.start()
     whole[rows_of(col, col_chunk), :] = gathered[...]
 
-    def take(one, has, src, rows, cols):
+    def take(halo, src, parts_of):
+        one, _, has = halo
+        rows, cols = src.shape[1:]
+
         @pl.when(has)
         def _():
             one.wait_recv()
-            for c in range(2):
+            for c in parts_of:
                 sample_out[c, :rows, :cols] -= src[c].astype(f32) * scale
 
-    take(halos[0][0], halos[0][2], from_left, *from_left.shape[1:])
-    take(halos[1][0], halos[1][2], from_above, *from_above.shape[1:])
-    take(halos[2][0], halos[2][2], from_both, *from_both.shape[1:])
+    take(halos[1], from_above, (0,))
+    take(halos[0], from_left, (0, 1))
+    take(halos[2], from_above, (1,))
+    take(halos[3], from_both, (0, 1))
 
     for one in gather_cols:
         one.wait_recv()
@@ -471,7 +479,7 @@
             pltpu.VMEM((row_chunk, LANES), bf16),
             pltpu.VMEM((col_chunk, LANES), bf16),
             pltpu.VMEM((lines, LANES), bf16),
-            dma((3,)), dma((3,)),
+            dma((4,)), dma((4,)),
             dma((n_col,)), dma((n_col,)), dma((n_row,)), dma((n_row,)),
             dma((n_row,)), dma((n_row,)), dma((n_col,)), dma((n_col,)),
         ],

time: 93.6 us -> 88.7 us (0.948); the launches traced: 93 us -> 89.5 us
  Pallas kernels: 85.2 us -> 81.7 us
    pallas_call x1, Pallas kernels: 50.1 us -> 46.5 us  [shards(): pl.pallas_call(functools.partial(exchange_kernel, n_row=n_row, n_col=n_co...]
where the time goes in v5:
time: 88.7 us; the launch traced here: 89.5 us
  Pallas kernels  81.7 us (92%)
  local copies, waits for them, and re-layouts  6.49 us (7%)
  between operations  1.32 us (1%)
    pallas_call x1, Pallas kernels, shards(): pl.pallas_call(functools.partial(exchange_kernel, n_row=n_row, n_col=n_co...  46.5 us
    pallas_call x1, Pallas kernels, shards(): pl.pallas_call(functools.partial(halo_kernel, n_row=n_row, n_col=n_col),...  20.6 us
    pallas_call x1, Pallas kernels, shards(): pl.pallas_call(gradient_kernel, out_shape=(shape((2, rows, cols), f32), s...  14.6 us
    unnamed x9, local copies, waits for them, and re-layouts  6.4 us

profile of v5, /device:TPU:0, one launch (start us, length us, event | category | flops | bytes accessed | tf_op | source)
XLA Modules:
  0.0 89.5 jit_solution(8079633496885825340)
XLA Ops:
  1.3 0.8 copy.9
  2.0 0.1 reshape.13.offsets
  2.1 0.0 copy-start
  2.1 1.6 %copy-done = f32[2,512,512]{2,1,0:T(8,128)S(1)} copy-done((f32[2,512,512]{2,1,0:T(8,128)S(1)}, f32[2,512,512]{2,1,0:T(8,128)}, u32[]{:S(2)}) %copy-start) | copy-done | bytes 2097176
  3.7 0.0 copy-start.1
  3.7 0.0 copy-start.2
  3.7 20.6 %shard_map.77 = (bf16[2,512,256]{2,1,0:T(8,128)(2,1)S(1)}, bf16[2,256,512]{2,1,0:T(8,128)(2,1)S(1)}, bf16[2,256,256]{2,1,0:T(8,128)(2,1)S(1)}) custom-call(f32[2,512,512]{2,1,0:T(8,128)S(1)} %copy-done), custom_call_target="tpu_custom_call" | custom-call | tf_op jit(solution)/shard_map/pallas_call | solution.py:426
  24.3 0.0 copy-done.1
  24.3 0.0 copy-done.2
  24.3 14.6 %shard_map.78 = (f32[2,512,512]{2,1,0:T(8,128)}, bf16[2,512,256]{2,1,0:T(8,128)(2,1)S(1)}, bf16[2,256,512]{2,1,0:T(8,128)(2,1)S(1)}, bf16[2,256,256]{2,1,0:T(8,128)(2,1)S(1)}, f32[2,2,256,256]{3,2,1,0:T(8,128)S(1)}) custom-call(s32[32]{0:T(128)S(1)} %reshape.13.offsets, s32[1]{0:T(128)} %bitcast.4.counts, bf16[6,256,256]{2,1,0:T(8,128)(2,1)S(1)} %copy-done.2, ...), custom_call_target="tpu_custom_call" | custom-call | tf_op jit(solution)/shard_map/pallas_call | solution.py:436
  39.0 46.5 %shard_map.79 = (f32[2,512,512]{2,1,0:T(8,128)}, f32[2,2,256,256]{3,2,1,0:T(8,128)S(1)}) custom-call(f32[2,512,512]{2,1,0:T(8,128)} %sample.5, f32[2,512,512]{2,1,0:T(8,128)} %get-tuple-element.13.main, bf16[2,512,256]{2,1,0:T(8,128)(2,1)S(1)} %get-tuple-element.14.right_grad, bf16[2,256,512]{2,1,0:T(8,128)(2,1)S(1)} %get-tuple-element.15.below_grad, ...), custom_call_target="tpu_custom_call" | custom-call | tf_op jit(solution)/shard_map/pallas_call | solution.py:464
  85.5 3.1 %copy.13 = f32[2,512,512]{2,1,0:T(8,128)} copy(f32[2,512,512]{2,1,0:T(8,128)} %get-tuple-element.20) | data formatting | bytes 4194304
  88.6 1.0 %copy.14 = f32[2,2,256,256]{3,2,1,0:T(8,128)} copy(f32[2,2,256,256]{3,2,1,0:T(8,128)S(1)} %get-tuple-element.21) | data formatting | bytes 2097152
Async XLA Ops:
  2.1 1.6 %copy-start = (f32[2,512,512]{2,1,0:T(8,128)S(1)}, f32[2,512,512]{2,1,0:T(8,128)}, u32[]{:S(2)}) copy-start(f32[2,512,512]{2,1,0:T(8,128)} %sample.5) | copy-start | bytes 6291460
  3.7 20.6 %copy-start.1 = (f32[2,2,256,256]{3,2,1,0:T(8,128)S(1)}, f32[2,2,256,256]{3,2,1,0:T(8,128)}, u32[]{:S(2)}) copy-start(f32[2,2,256,256]{3,2,1,0:T(8,128)} %probe.3) | copy-start | bytes 3145732
  3.7 20.6 %copy-start.2 = (bf16[6,256,256]{2,1,0:T(8,128)(2,1)S(1)}, bf16[6,256,256]{2,1,0:T(8,128)(2,1)}, u32[]{:S(2)}) copy-start(bf16[6,256,256]{2,1,0:T(8,128)(2,1)} %constant.2.clone.table) | copy-start | bytes 2359300

commit v6 on v5

--- a/solution.py
+++ b/solution.py
@@ -371,8 +371,6 @@
     gathered[rows_of(row, row_chunk), :] = row_sum[...]
     for one in gather_rows:
         one.wait_recv()
-    for one, gives, _ in halos[2:]:
-        pl.when(gives)(one.start)
     gather_cols = [
         copy(
             gathered, whole.at[rows_of(col, col_chunk)],
@@ -382,6 +380,8 @@
     ]
     for one in gather_cols:
         one.start()
+    for one, gives, _ in halos[2:]:
+        pl.when(gives)(one.start)
     whole[rows_of(col, col_chunk), :] = gathered[...]
 
     def take(halo, src, parts_of):

time: 88.7 us -> 89.6 us (1.010); the launches traced: 89.5 us -> 89.4 us
    pallas_call x1, Pallas kernels: 14.6 us -> 7.29 us  [shards(): pl.pallas_call(gradient_kernel, out_shape=(shape((2, rows, cols), f32), s...]
    pallas_call x1, Pallas kernels: 46.5 us -> 53.7 us  [shards(): pl.pallas_call(functools.partial(exchange_kernel, n_row=n_row, n_col=n_co...]
where the time goes in v6:
time: 89.6 us; the launch traced here: 89.4 us
  Pallas kernels  81.6 us (91%)
  local copies, waits for them, and re-layouts  6.49 us (7%)
  between operations  1.32 us (1%)
    pallas_call x1, Pallas kernels, shards(): pl.pallas_call(functools.partial(exchange_kernel, n_row=n_row, n_col=n_co...  53.7 us
    pallas_call x1, Pallas kernels, shards(): pl.pallas_call(functools.partial(halo_kernel, n_row=n_row, n_col=n_col),...  20.6 us
    pallas_call x1, Pallas kernels, shards(): pl.pallas_call(gradient_kernel, out_shape=(shape((2, rows, cols), f32), s...  7.29 us
    unnamed x9, local copies, waits for them, and re-layouts  6.4 us

profile of v6, /device:TPU:0, one launch (start us, length us, event | category | flops | bytes accessed | tf_op | source)
XLA Modules:
  0.0 89.4 jit_solution(10010179040529307558)
XLA Ops:
  1.3 0.8 copy.9
  2.0 0.1 reshape.13.offsets
  2.1 0.0 copy-start
  2.1 1.6 %copy-done = f32[2,512,512]{2,1,0:T(8,128)S(1)} copy-done((f32[2,512,512]{2,1,0:T(8,128)S(1)}, f32[2,512,512]{2,1,0:T(8,128)}, u32[]{:S(2)}) %copy-start) | copy-done | bytes 2097176
  3.7 0.0 copy-start.1
  3.7 0.0 copy-start.2
  3.7 20.6 %shard_map.77 = (bf16[2,512,256]{2,1,0:T(8,128)(2,1)S(1)}, bf16[2,256,512]{2,1,0:T(8,128)(2,1)S(1)}, bf16[2,256,256]{2,1,0:T(8,128)(2,1)S(1)}) custom-call(f32[2,512,512]{2,1,0:T(8,128)S(1)} %copy-done), custom_call_target="tpu_custom_call" | custom-call | tf_op jit(solution)/shard_map/pallas_call | solution.py:426
  24.3 0.0 copy-done.1
  24.3 0.0 copy-done.2
  24.3 7.3 %shard_map.78 = (f32[2,512,512]{2,1,0:T(8,128)}, bf16[2,512,256]{2,1,0:T(8,128)(2,1)S(1)}, bf16[2,256,512]{2,1,0:T(8,128)(2,1)S(1)}, bf16[2,256,256]{2,1,0:T(8,128)(2,1)S(1)}, f32[2,2,256,256]{3,2,1,0:T(8,128)S(1)}) custom-call(s32[32]{0:T(128)S(1)} %reshape.13.offsets, s32[1]{0:T(128)} %bitcast.4.counts, bf16[6,256,256]{2,1,0:T(8,128)(2,1)S(1)} %copy-done.2, ...), custom_call_target="tpu_custom_call" | custom-call | tf_op jit(solution)/shard_map/pallas_call | solution.py:436
  31.6 53.7 %shard_map.79 = (f32[2,512,512]{2,1,0:T(8,128)}, f32[2,2,256,256]{3,2,1,0:T(8,128)S(1)}) custom-call(f32[2,512,512]{2,1,0:T(8,128)} %sample.5, f32[2,512,512]{2,1,0:T(8,128)} %get-tuple-element.13.main, bf16[2,512,256]{2,1,0:T(8,128)(2,1)S(1)} %get-tuple-element.14.right_grad, bf16[2,256,512]{2,1,0:T(8,128)(2,1)S(1)} %get-tuple-element.15.below_grad, ...), custom_call_target="tpu_custom_call" | custom-call | tf_op jit(solution)/shard_map/pallas_call | solution.py:464
  85.4 3.1 %copy.13 = f32[2,512,512]{2,1,0:T(8,128)} copy(f32[2,512,512]{2,1,0:T(8,128)} %get-tuple-element.20) | data formatting | bytes 4194304
  88.4 1.0 %copy.14 = f32[2,2,256,256]{3,2,1,0:T(8,128)} copy(f32[2,2,256,256]{3,2,1,0:T(8,128)S(1)} %get-tuple-element.21) | data formatting | bytes 2097152
Async XLA Ops:
  2.1 1.6 %copy-start = (f32[2,512,512]{2,1,0:T(8,128)S(1)}, f32[2,512,512]{2,1,0:T(8,128)}, u32[]{:S(2)}) copy-start(f32[2,512,512]{2,1,0:T(8,128)} %sample.5) | copy-start | bytes 6291460
  3.7 20.6 %copy-start.1 = (f32[2,2,256,256]{3,2,1,0:T(8,128)S(1)}, f32[2,2,256,256]{3,2,1,0:T(8,128)}, u32[]{:S(2)}) copy-start(f32[2,2,256,256]{3,2,1,0:T(8,128)} %probe.3) | copy-start | bytes 3145732
  3.7 20.6 %copy-start.2 = (bf16[6,256,256]{2,1,0:T(8,128)(2,1)S(1)}, bf16[6,256,256]{2,1,0:T(8,128)(2,1)}, u32[]{:S(2)}) copy-start(bf16[6,256,256]{2,1,0:T(8,128)(2,1)} %constant.2.clone.table) | copy-start | bytes 2359300
